TPU v7x, 512 devices: a whole 4x4x16 slice. The times are simulated.
512 devices in a mesh: dp: 4 (over y), ctx: 64 (over x, z), mp: 2 (over core).
Axes of the slice: x: 4, y: 4, z: 16, core: 2. Of those that a mesh axis runs over, the one named last changes fastest.
Arguments:
- features: bfloat16 [4, 8192, 3, 4096], P('dp', 'ctx', None, 'mp'), may hold values from -6 to 6
- conv_weight: float32 [7, 3, 4096], P(None, None, 'mp'), may hold values from -2 to 2
- log_rate: float32 [8, 32], P(None, 'mp'), as said below
- residues: float32 [8, 4096], P(None, 'mp'), may hold values from -4 to 4
- skip_weight: float32 [4096], P('mp'), may hold values from 0.5 to 1.5
- norm_gain: float32 [4096], P('mp'), may hold values from 0.5 to 1.5
- cotangent: bfloat16 [4, 8192, 4096], P('dp', 'ctx', 'mp'), may hold values from -6 to 6
Outputs:
- block_out: bfloat16 [4, 8192, 4096], P('dp', 'ctx', 'mp')
- feature_grad: bfloat16 [4, 8192, 3, 4096], P('dp', 'ctx', None, 'mp')
- conv_grad: float32 [7, 3, 4096], P(None, None, 'mp')
- rate_grad: float32 [8, 32], P(None, 'mp')
- residue_grad: float32 [8, 4096], P(None, 'mp')
- skip_grad: float32 [4096], P('mp')
- gain_grad: float32 [4096], P('mp')
Inputs may be any that keep to these rules, and one draw needn't show every extreme that they name: log_rate lies between ln(1 / 1048576) and ln(1 / 16).
All inputs are finite; a program needn't handle non-finite values.
Results may differ from a plain program's by a relative error of at most 0.0011.
Values may be sent and summed in bfloat16 or wider, within the bound.
No kernel may reach another device: no remote copies, remote signals or barrier semaphores. Data moves between devices by JAX's collectives and lax.ppermute only.
A program may use at most 128 MiB of HBM per device.

v0:
```python
import jax
import jax.numpy as jnp
from jax import lax
from jax.sharding import PartitionSpec as P

D = 4096
EPSILON = 1e-06
HIGHEST = lax.Precision.HIGHEST


def passed_along(value, axis, steps):
    count = lax.axis_size(axis)
    leading, last = (max(0, -steps), min(count, count - steps))
    return lax.ppermute(value, axis, [(source, source + steps) for source in range(leading, last)])


def carried_in(part, axis, combine, identity, reverse):
    count = lax.axis_size(axis)
    place = lax.axis_index(axis)
    ahead = count - 1 - place if reverse else place
    gathered = jax.tree.map(lambda a: lax.all_gather(a, axis), part)
    state = jax.tree.map(lambda a, e: jnp.zeros_like(a) + jnp.asarray(e, a.dtype), part, identity)

    def one(lap, state):
        source = count - 1 - lap if reverse else lap
        return combine(
            state, jax.tree.map(lambda a: lax.dynamic_index_in_dim(a, source, 0, False), gathered)
        )

    return lax.fori_loop(0, ahead, one, state)


def decay_matrix(rate_row, length):
    places = jnp.arange(length, dtype=jnp.float32)
    lagged = places[:, None] - places[None, :]
    clipped = jnp.maximum(lagged, 0.0)
    matrix = jnp.where(lagged >= 0, jnp.exp(-rate_row[:, None, None] * clipped), 0.0)
    return (matrix, clipped)


def compose_back(earlier, later):
    return (earlier[0] * later[0], earlier[1] * later[0][..., None] + later[1])


def local(features, conv_weight, log_rate, residues, skip_weight, norm_gain, cotangent):
    local_feats = features[0]
    length = local_feats.shape[0]
    channels = local_feats.shape[2]
    pole_count = log_rate.shape[0]
    groups_here = log_rate.shape[1]
    group_size = channels // groups_here
    halo_rows = conv_weight.shape[0] - 1
    previous = passed_along(local_feats[length - halo_rows :], "ctx", 1)
    extended = jnp.concatenate([previous, local_feats], axis=0)
    filtered = conv_weight[0] * extended[halo_rows : halo_rows + length]
    for offset in range(1, halo_rows + 1):
        filtered = (
            filtered
            + conv_weight[offset] * extended[halo_rows - offset : halo_rows - offset + length]
        )
    query_rows = filtered[:, 0]
    key_rows = filtered[:, 1]
    value_rows = filtered[:, 2]
    product = key_rows * value_rows
    rate_rows = jnp.exp(log_rate).T
    grouped = product.reshape(length, groups_here, group_size).transpose(1, 0, 2)
    places = jnp.arange(length, dtype=jnp.float32)
    tail_lag = length - 1.0 - places
    block_decay = jnp.exp(-rate_rows * length)

    def forward_plain(pieces):
        rate_row, product_block = pieces
        matrix, clipped = decay_matrix(rate_row, length)
        return jnp.einsum("pts,sc->ptc", matrix, product_block, precision=HIGHEST)

    local_states = lax.map(forward_plain, (rate_rows, grouped))
    end_rows = local_states[:, :, length - 1, :]
    carried = carried_in(
        (block_decay, end_rows),
        "ctx",
        compose_back,
        (jnp.ones_like(block_decay), jnp.zeros_like(end_rows)),
        False,
    )
    state_in = carried[1]
    head_decay = jnp.exp(-rate_rows[:, :, None] * (places + 1.0))
    states = local_states + head_decay[..., None] * state_in[:, :, None, :]
    weights = residues.reshape(pole_count, groups_here, group_size).transpose(1, 0, 2)
    modal_part = jnp.einsum("gptc,gpc->tgc", states, weights, precision=HIGHEST).reshape(
        length, channels
    )
    branch = modal_part + skip_weight * product
    gated_rows = query_rows * branch
    seed_grad = cotangent[0].astype(jnp.float32)
    scaled_grad = norm_gain * seed_grad
    square_sum = lax.psum(jnp.sum(gated_rows * gated_rows, axis=1), "mp")
    inv_rms = lax.rsqrt(square_sum / D + EPSILON)[:, None]
    normed = gated_rows * inv_rms
    block_out = (norm_gain * normed).astype(jnp.bfloat16)
    slope_sum = lax.psum(jnp.sum(scaled_grad * gated_rows, axis=1), "mp")
    gain_local = jnp.sum(seed_grad * normed, axis=0)
    dgated = scaled_grad * inv_rms - gated_rows * (
        slope_sum[:, None] * inv_rms * inv_rms * inv_rms / D
    )
    dquery = dgated * branch
    dbranch = dgated * query_rows
    skip_local = jnp.sum(dbranch * product, axis=0)
    dgrouped = dbranch.reshape(length, groups_here, group_size).transpose(1, 0, 2)
    back_in = jnp.einsum("gpt,gtc->gpc", head_decay, dgrouped, precision=HIGHEST)
    returned = carried_in(
        (block_decay, back_in),
        "ctx",
        compose_back,
        (jnp.ones_like(block_decay), jnp.zeros_like(back_in)),
        True,
    )
    later_in = returned[1]

    def backward_adjoint(pieces):
        (
            rate_row,
            product_block,
            grad_block,
            state_block,
            weight_row,
            later_row,
            start_row,
            slope_row,
        ) = pieces
        matrix, clipped = decay_matrix(rate_row, length)
        residue_part = jnp.sum(grad_block[None] * state_block, axis=1)
        tail_row = jnp.exp(-rate_row[:, None] * tail_lag)
        adjoint = (
            jnp.einsum("pts,tc->psc", matrix, grad_block, precision=HIGHEST)
            + tail_row[..., None] * later_row[:, None, :]
        )
        inner = (
            jnp.sum(adjoint[:, 1:, :] * state_block[:, : length - 1, :], axis=1)
            + adjoint[:, 0, :] * start_row
        )
        rate_part = -jnp.exp(-rate_row) * jnp.sum(weight_row * inner, axis=1)
        return (residue_part, rate_part, jnp.sum(weight_row[:, None, :] * adjoint, axis=0))

    residue_parts, rate_parts, dproduct_groups = lax.map(
        backward_adjoint,
        (rate_rows, grouped, dgrouped, states, weights, later_in, state_in, state_in),
    )
    residue_local = residue_parts.transpose(1, 0, 2).reshape(pole_count, channels)
    rate_local = rate_parts.T * jnp.exp(log_rate)
    dproduct = dproduct_groups.transpose(1, 0, 2).reshape(length, channels) + dbranch * skip_weight
    dfiltered = jnp.stack([dquery, dproduct * value_rows, dproduct * key_rows], axis=1)
    zeros_rim = jnp.zeros((halo_rows, 3, channels), jnp.float32)
    padded_grad = jnp.concatenate([zeros_rim, dfiltered, zeros_rim], axis=0)
    dextended = conv_weight[0] * padded_grad[0 : length + halo_rows]
    for offset in range(1, halo_rows + 1):
        dextended = (
            dextended + conv_weight[offset] * padded_grad[offset : offset + length + halo_rows]
        )
    conv_local = jnp.stack(
        [
            jnp.sum(dfiltered * extended[halo_rows - offset : halo_rows - offset + length], axis=0)
            for offset in range(halo_rows + 1)
        ],
        axis=0,
    )
    incoming = passed_along(dextended[:halo_rows], "ctx", -1)
    dlocal = dextended[halo_rows:] + jnp.concatenate(
        [jnp.zeros((length - halo_rows, 3, channels), jnp.float32), incoming], axis=0
    )
    feature_grad = dlocal.astype(jnp.bfloat16)[None]
    totals = lax.psum(
        (conv_local, rate_local, residue_local, skip_local, gain_local), ("dp", "ctx")
    )
    return (block_out[None], feature_grad, totals[0], totals[1], totals[2], totals[3], totals[4])


def solution(mesh):
    in_specs = (
        P("dp", "ctx", None, "mp"),
        P(None, None, "mp"),
        P(None, "mp"),
        P(None, "mp"),
        P("mp"),
        P("mp"),
        P("dp", "ctx", "mp"),
    )
    out_specs = (
        P("dp", "ctx", "mp"),
        P("dp", "ctx", None, "mp"),
        P(None, None, "mp"),
        P(None, "mp"),
        P(None, "mp"),
        P("mp"),
        P("mp"),
    )
    return jax.shard_map(local, mesh=mesh, in_specs=in_specs, out_specs=out_specs, check_vma=False)
```

profile of v0, /device:TPU:0, one launch (start us, length us, event | category | flops | bytes accessed | tf_op | source)
XLA Modules:
  0.0 2139.7 jit_solution(14530745588208930304)
XLA Ops:
  9.4 2.1 fusion.91
  12.5 7.9 fusion.48
  23.7 1.3 copy.102
  25.0 38.0 %while.51 = (s32[]{:T(128)}, f32[16,8,128,128]{3,2,1,0:T(8,128)}, f32[16,8]{1,0:T(8,128)S(1)}, f32[16,128,128]{2,1,0:T(8,128)}, s32[]{:T(128)}) while((s32[]{:T(128)}, f32[16,8,128,128]{3,2,1,0:T(8,128)}, f32[16,8]{1,0:T(8,128)S(1)}, f32[16,128,128]{2,1,0:T(8,128)}, s32[]{:T(128)}) %tuple.143), condition=%wide.region_1.2_spmd, body=%wide.region_0.1_spmd.sunk | while | flops 201654288 | bytes 754849 | solution.py:76
  25.1 2.3 fusion.110
  27.5 2.3 fusion.110
  29.9 2.3 fusion.110
  32.3 2.3 fusion.110
  34.6 2.3 fusion.110
  37.0 2.3 fusion.110
  39.4 2.3 fusion.110
  41.7 2.3 fusion.110
  44.1 2.3 fusion.110
  46.5 2.3 fusion.110
  48.9 2.3 fusion.110
  51.3 2.3 fusion.110
  53.6 2.3 fusion.110
  56.0 2.3 fusion.110
  58.3 2.3 fusion.110
  60.7 2.3 fusion.110
  63.0 9.9 copy.50
  76.2 91.5 %all-gather.3 = f32[64,16,8]{1,2,0:T(8,128)} all-gather(f32[1,16,8]{1,2,0:T(8,128)S(1)} %get-tuple-element.392), channel_id=2, replica_groups=mesh['dp'=4,'ctx'=64,'mp'=2] {'ctx'}, dimensions={0}, use_global_device_ids=true | all-gather | bytes 33280 | tf_op jit(solution)/shard_map/all_gather | solution.py:21
  169.1 53.8 %all-gather.7.cloned.1.call-done = f32[1024,8,1,128]{3,1,2,0:T(8,128)} async-done(((f32[16,8,1,128]{3,1,2,0:T(8,128)}), f32[1024,8,1,128]{3,1,2,0:T(8,128)}) %all-gather.7.cloned.1.call-update) | async-done | bytes 4194320 | tf_op jit(solution)/shard_map/all_gather | solution.py:21
  223.0 8.3 multiply_reduce_fusion.2
  231.3 1.3 fusion.67
  232.6 2.5 all-reduce.5
  235.1 3.2 fusion.85
  239.3 1.6 fusion.87
  241.1 2.9 copy.51
  243.9 2.4 reshape.384
  246.3 2.4 reshape.382
  248.7 2.9 fusion.72
  252.8 232.8 %all-gather.9.cloned.1.call-done = f32[1024,8,128]{2,1,0:T(8,128)} async-done(((f32[16,8,128]{2,1,0:T(8,128)}), f32[1024,8,128]{2,1,0:T(8,128)}) %all-gather.9.cloned.1.call-update) | async-done | bytes 4194320 | tf_op jit(solution)/shard_map/all_gather | solution.py:21
  485.6 107.9 %while.53 = (s32[]{:T(128)}, f32[16,8,128]{2,1,0:T(8,128)S(1)}, s32[]{:T(128)}, f32[64,16,8]{1,2,0:T(8,128)}, f32[64,16,8,128]{3,2,1,0:T(8,128)}, /*index=5*/s32[]{:T(128)}, s32[]{:T(128)}, s32[]{:T(128)}, s32[]{:T(128)}) while((s32[]{:T(128)}, f32[16,8,128]{2,1,0:T(8,128)S(1)}, s32[]{:T(128)}, f32[64,16,8]{1,2,0:T(8,128)}, ...), condition=%wide.region_9.10_spmd, body=%wide.region_8.9_spmd.sunk | while | flops 32774 | bytes 199315 | solution.py:30
  594.1 146.1 %while.54 = (s32[]{:T(128)}, f32[16,8,128]{2,1,0:T(8,128)}, f32[16,8]{1,0:T(8,128)}, f32[16,128,128]{2,1,0:T(8,128)}, f32[16,128,128]{2,1,0:T(8,128)}, /*index=5...) while((s32[]{:T(128)}, f32[16,8,128]{2,1,0:T(8,128)}, ...), condition=%wide.region_15.16_spmd.clone, body=%wide.region_10.15_spmd.clone.sunk | while | flops 202687648 | bytes 3312593 | solution.py:144
  595.6 1.5 multiply_reduce_fusion.7
  604.8 1.5 multiply_reduce_fusion.7
  610.5 1.3 dynamic_update_slice.29
  613.9 1.5 multiply_reduce_fusion.7
  623.1 1.5 multiply_reduce_fusion.7
  628.7 1.3 dynamic_update_slice.29
  632.2 1.5 multiply_reduce_fusion.7
  641.3 1.5 multiply_reduce_fusion.7
  650.4 1.5 multiply_reduce_fusion.7
  659.6 1.5 multiply_reduce_fusion.7
  668.7 1.5 multiply_reduce_fusion.7
  677.8 1.5 multiply_reduce_fusion.7
  686.9 1.5 multiply_reduce_fusion.7
  696.1 1.5 multiply_reduce_fusion.7
  705.2 1.5 multiply_reduce_fusion.7
  714.3 1.5 multiply_reduce_fusion.7
  723.5 1.5 multiply_reduce_fusion.7
  732.6 1.5 multiply_reduce_fusion.7
  740.2 1.4 copy.60
  741.6 2.8 copy.59
  744.4 2.4 reshape.385
  746.8 2.9 slice_multiply_fusion.6
  751.2 3.4 fusion.54
  755.3 2.8 fusion.38
  758.1 1.7 copy-done.5
  762.0 1364.5 %all-reduce.3 = (f32[8,16]{1,0:T(8,128)}, f32[2048]{0:T(1024)}, f32[2048]{0:T(1024)}) all-reduce(f32[8,16]{1,0:T(8,128)S(1)} %bitcast_multiply_fusion.4, f32[2048]{0:T(1024)} %get-tuple-element.308, f32[2048]{0:T(1024)S(1)} %copy-done.24), channel_id=1, replica_groups=mesh['dp'=4,'ctx'=64,'mp'=2] {'dp','ctx'}, use_global_device_ids=true, to_apply=%region_24.25 | all-reduce | flops 4224 | bytes 33792 | tf_op jit(solution)/shard_map/psum | solution.py:171
  2126.5 3.5 fusion.57
  2130.0 1.7 copy.61
  2131.7 1.5 copy.150
  (590 shorter events, 244.1 us)
Async XLA Ops:
  7.2 215.7 %all-gather.7.cloned.1.call-start = ((), (), s32[]{:S(2)}) async-start(), calls=%async_computation | async-start | bytes 4259840 | tf_op jit(solution)/shard_map/all_gather | solution.py:21
  8.1 4.3 collective-permute-start
  11.6 9.9 copy-start.12
  12.4 9.1 copy-start.14
  21.5 1.0 copy-start
  22.7 1.0 copy-start.6
  63.0 10.0 copy-start.26
  63.0 10.7 copy-start.23
  73.6 411.9 %all-gather.9.cloned.1.call-start = ((), (), s32[]{:S(2)}) async-start(), calls=%async_computation.1 | async-start | bytes 4259840 | tf_op jit(solution)/shard_map/all_gather | solution.py:21
  73.8 149.1 %copy-start.21 = (f32[16,8]{1,0:T(8,128)}, f32[16,8]{1,0:T(8,128)S(1)}, u32[]{:S(2)}) copy-start(f32[16,8]{1,0:T(8,128)S(1)} %copy.49) | copy-start | bytes 1540
  73.8 94.1 %copy-start.9 = (f32[16,8,16,128]{3,1,2,0:T(8,128)S(1)}, f32[16,8,16,128]{3,1,2,0:T(8,128)}, u32[]{:S(2)}) copy-start(f32[16,8,16,128]{3,1,2,0:T(8,128)} %get-tuple-element.382) | copy-start | bytes 3145732
  167.8 55.1 %copy-start.31 = (f32[128]{0:T(128)}, f32[128]{0:T(128)S(1)}, u32[]{:S(2)}) copy-start(f32[128]{0:T(128)S(1)} %iota_add_fusion) | copy-start | bytes 1540
  222.9 8.3 copy-start.1
  222.9 8.3 copy-start.7
  222.9 8.3 copy-start.16
  222.9 8.3 copy-start.18
  231.2 1.4 copy-start.3
  231.2 3.9 copy-start.19
  232.6 6.7 copy-start.22
  232.6 6.7 copy-start.32
  235.1 13.6 copy-start.29
  235.1 16.5 copy-start.27
  238.3 1.1 copy-start.8
  241.0 1888.9 %all-reduce.8.cloned.1.call-start = ((), (), s32[]{:S(2)}) async-start(), calls=%async_computation.2 | async-start | bytes 589824 | tf_op jit(solution)/shard_map/psum | solution.py:171
  248.7 2.9 copy-start.2
  248.7 2.9 copy-start.10
  740.2 6.6 copy-start.17
  740.2 6.6 copy-start.20
  740.2 6.6 copy-start.28
  740.2 6.6 copy-start.30
  749.8 1.4 copy-start.4
  754.6 0.8 copy-start.13
  754.6 0.8 copy-start.15
  755.3 6.6 copy-start.25
  755.3 6.7 copy-start.24
  758.1 1.7 copy-start.5
  759.8 1366.6 %collective-permute-start.1 = (f32[6,3,2048]{2,0,1:T(8,128)S(1)}, f32[6,3,2048]{2,0,1:T(8,128)S(1)}, u32[]{:S(2)}, u32[]{:S(2)}) collective-permute-start(f32[6,3,2048]{2,0,1:T(8,128)S(1)} %slice.156), channel_id=1, source_target_pairs={{2,0},{4,2},{6,4},{8,6},{10,8},{12,10},{14,12},{16,14},{18,16},{20... | collective-permute-start | bytes 442376 | tf_op jit(solution)/shard_map/ppermute | solution.py:14
  761.3 0.7 copy-start.11
Sparse Core Ops, SparseCore 0:
  73.8 149.0 all-gather.6
  241.1 244.3 all-gather.8
  762.1 380.4 all-reduce.7
where the time goes:
time: 2150 us; the launch traced here: 2140 us
  blocking collectives  1460 us (68%)
  waiting for transfers between devices  287 us (13%)
  local copies, waits for them, and re-layouts  156 us (7%)
  other arithmetic  156 us (7%)
  matrix products  62.4 us (3%)
    psum x1, blocking collectives, local(): lax.psum((conv_local, rate_local, residue_local, skip_local, gain_local),...  1360 us
    all_gather x2, waiting for transfers between devices, carried_in(): gathered = jax.tree.map(lambda a: lax.all_gather(a, axis), part)  287 us
    all_gather x1, blocking collectives, carried_in(): gathered = jax.tree.map(lambda a: lax.all_gather(a, axis), part)  91.5 us
    add x63, other arithmetic, compose_back(): return (earlier[0] * later[0], earlier[1] * later[0][..., None] + later[1])  58.2 us
    mul x126, local copies, waits for them, and re-layouts, compose_back(): return (earlier[0] * later[0], earlier[1] * later[0][..., None] + later[1])  47.7 us
  transfers between devices with their start and end apart: 5, of which 2 were waited for; matrix products, arithmetic and copies ran while one was open for 1% of the time, Pallas kernels for 0%

commit v1 on v0

--- a/solution.py
+++ b/solution.py
@@ -169,7 +169,7 @@
     )
     feature_grad = dlocal.astype(jnp.bfloat16)[None]
     totals = lax.psum(
-        (conv_local, rate_local, residue_local, skip_local, gain_local), ("dp", "ctx")
+        lax.psum((conv_local, rate_local, residue_local, skip_local, gain_local), "ctx"), "dp"
     )
     return (block_out[None], feature_grad, totals[0], totals[1], totals[2], totals[3], totals[4])
 

time: 2150 us -> 1100 us (0.51)
  blocking collectives: 1460 us -> 389 us
  waiting for transfers between devices: 287 us -> 327 us
    psum x1, blocking collectives: 1360 us -> 277 us  [local(): lax.psum((conv_local, rate_local, residue_local, skip_local, gain_local),...]
    psum x0 -> x1, waiting for transfers between devices: none -> 41.1 us  [local(): lax.psum(lax.psum((conv_local, rate_local, residue_local, skip_local, gai...]
  transfers between devices with their start and end apart: 5 -> 6, of which waited for: 2 -> 3; matrix products, arithmetic and copies ran while one was open for 1% -> 3% of each run, Pallas kernels for 0% -> 0%
where the time goes in v1:
time: 1100 us; the launch traced here: 1090 us
  blocking collectives  389 us (35%)
  waiting for transfers between devices  327 us (30%)
  other arithmetic  154 us (14%)
  local copies, waits for them, and re-layouts  136 us (12%)
  matrix products  62.4 us (6%)
  between operations  14.1 us (1%)
    all_gather x2, waiting for transfers between devices, carried_in(): gathered = jax.tree.map(lambda a: lax.all_gather(a, axis), part)  286 us
    psum x1, blocking collectives, local(): lax.psum((conv_local, rate_local, residue_local, skip_local, gain_local),...  277 us
    all_gather x1, blocking collectives, carried_in(): gathered = jax.tree.map(lambda a: lax.all_gather(a, axis), part)  92.1 us
    add x63, other arithmetic, compose_back(): return (earlier[0] * later[0], earlier[1] * later[0][..., None] + later[1])  58.2 us
    mul x126, local copies, waits for them, and re-layouts, compose_back(): return (earlier[0] * later[0], earlier[1] * later[0][..., None] + later[1])  47.7 us
    psum x1, waiting for transfers between devices, local(): lax.psum(lax.psum((conv_local, rate_local, residue_local, skip_local, gai...  41.1 us
    dot_general x16, matrix products, forward_plain(): return jnp.einsum('pts,sc->ptc', matrix, product_block, precision=HIGHEST)  36.8 us
    dynamic_update_slice x48, local copies, waits for them, and re-layouts, local(): lax.map(backward_adjoint, (rate_rows, grouped, dgrouped, states, weights,...  30.8 us
  transfers between devices with their start and end apart: 6, of which 3 were waited for; matrix products, arithmetic and copies ran while one was open for 3% of the time, Pallas kernels for 0%

profile of v1, /device:TPU:0, one launch (start us, length us, event | category | flops | bytes accessed | tf_op | source)
XLA Modules:
  0.0 1086.8 jit_solution(8587781748722761232)
XLA Ops:
  9.4 1.9 fusion.91
  12.3 7.5 fusion.48
  19.8 1.5 slice_bitcast_fusion
  25.1 38.0 %while.51 = (s32[]{:T(128)}, f32[16,8,128,128]{3,2,1,0:T(8,128)}, f32[16,8]{1,0:T(8,128)S(1)}, f32[16,128,128]{2,1,0:T(8,128)}, s32[]{:T(128)}) while((s32[]{:T(128)}, f32[16,8,128,128]{3,2,1,0:T(8,128)}, f32[16,8]{1,0:T(8,128)S(1)}, f32[16,128,128]{2,1,0:T(8,128)}, s32[]{:T(128)}) %tuple.146), condition=%wide.region_1.2_spmd, body=%wide.region_0.1_spmd.sunk | while | flops 201654288 | bytes 754849 | solution.py:76
  25.2 2.3 fusion.110
  27.6 2.4 fusion.110
  30.1 2.3 fusion.110
  32.4 2.3 fusion.110
  34.8 2.3 fusion.110
  37.2 2.3 fusion.110
  39.5 2.3 fusion.110
  41.9 2.3 fusion.110
  44.3 2.3 fusion.110
  46.7 2.3 fusion.110
  49.1 2.3 fusion.110
  51.4 2.3 fusion.110
  53.8 2.3 fusion.110
  56.1 2.3 fusion.110
  58.5 2.3 fusion.110
  60.9 2.3 fusion.110
  63.2 9.9 copy.50
  76.4 92.1 %all-gather.3 = f32[64,16,8]{1,2,0:T(8,128)} all-gather(f32[1,16,8]{1,2,0:T(8,128)S(1)} %get-tuple-element.397), channel_id=2, replica_groups=mesh['dp'=4,'ctx'=64,'mp'=2] {'ctx'}, dimensions={0}, use_global_device_ids=true | all-gather | bytes 33280 | tf_op jit(solution)/shard_map/all_gather | solution.py:21
  169.7 53.5 %all-gather.7.cloned.1.call-done = f32[1024,8,1,128]{3,1,2,0:T(8,128)} async-done(((f32[16,8,1,128]{3,1,2,0:T(8,128)}), f32[1024,8,1,128]{3,1,2,0:T(8,128)}) %all-gather.7.cloned.1.call-update) | async-done | bytes 4194320 | tf_op jit(solution)/shard_map/all_gather | solution.py:21
  223.3 9.2 multiply_reduce_fusion.2
  232.5 2.9 fusion.67
  235.4 2.4 all-reduce.7
  237.8 3.2 fusion.85
  242.1 1.6 fusion.87
  243.8 2.9 copy.51
  246.7 2.4 reshape.384
  249.0 2.4 reshape.382
  251.4 2.8 fusion.72
  254.2 2.4 fusion.81
  256.6 232.0 %all-gather.9.cloned.1.call-done = f32[1024,8,128]{2,1,0:T(8,128)} async-done(((f32[16,8,128]{2,1,0:T(8,128)}), f32[1024,8,128]{2,1,0:T(8,128)}) %all-gather.9.cloned.1.call-update) | async-done | bytes 4194320 | tf_op jit(solution)/shard_map/all_gather | solution.py:21
  488.6 107.7 %while.53 = (s32[]{:T(128)}, f32[16,8,128]{2,1,0:T(8,128)S(1)}, s32[]{:T(128)}, f32[64,16,8]{1,2,0:T(8,128)}, f32[64,16,8,128]{3,2,1,0:T(8,128)}, /*index=5*/s32[]{:T(128)}, s32[]{:T(128)}, s32[]{:T(128)}, s32[]{:T(128)}) while((s32[]{:T(128)}, f32[16,8,128]{2,1,0:T(8,128)S(1)}, s32[]{:T(128)}, f32[64,16,8]{1,2,0:T(8,128)}, ...), condition=%wide.region_9.10_spmd, body=%wide.region_8.9_spmd.sunk | while | flops 32774 | bytes 199315 | solution.py:30
  596.3 114.5 %while.54 = (s32[]{:T(128)}, f32[16,8,128]{2,1,0:T(8,128)S(1)}, f32[16,8]{1,0:T(8,128)}, f32[16,128,128]{2,1,0:T(8,128)}, f32[16,128,128]{2,1,0:T(8,128)}, /*ind...) while((s32[]{:T(128)}, f32[16,8,128]{2,1,0:T(8,128)S(1)}, ...), condition=%wide.region_15.16_spmd.clone, body=%wide.region_10.15_spmd.clone.sunk | while | flops 202687648 | bytes 3312085 | solution.py:144
  597.2 1.5 multiply_reduce_fusion.7
  604.3 1.5 multiply_reduce_fusion.7
  611.5 1.5 multiply_reduce_fusion.7
  618.7 1.5 multiply_reduce_fusion.7
  625.8 1.5 multiply_reduce_fusion.7
  633.0 1.5 multiply_reduce_fusion.7
  640.1 1.5 multiply_reduce_fusion.7
  647.3 1.5 multiply_reduce_fusion.7
  654.4 1.5 multiply_reduce_fusion.7
  661.6 1.5 multiply_reduce_fusion.7
  668.7 1.5 multiply_reduce_fusion.7
  675.9 1.5 multiply_reduce_fusion.7
  683.1 1.5 multiply_reduce_fusion.7
  690.2 1.5 multiply_reduce_fusion.7
  697.4 1.5 multiply_reduce_fusion.7
  704.5 1.5 multiply_reduce_fusion.7
  710.8 2.8 copy.59
  713.7 2.4 reshape.385
  716.0 2.7 slice_multiply_fusion.6
  718.8 2.0 pad_maximum_fusion.1
  720.9 3.4 fusion.54
  729.4 5.9 fusion.38
  738.3 276.7 %all-reduce.3 = (f32[8,16]{1,0:T(8,128)S(1)}, f32[2048]{0:T(1024)S(1)}, f32[2048]{0:T(1024)S(1)}) all-reduce(f32[8,16]{1,0:T(8,128)S(1)} %bitcast_multiply_fusion.4, f32[2048]{0:T(1024)} %get-tuple-element.308, f32[2048]{0:T(1024)S(1)} %get-tuple-element.307), channel_id=1, replica_groups=mesh['dp'=4,'ctx'=64,'mp'=2] {'ctx'}, use_global_device_ids=true, to_apply=%region_25.26 | all-reduce | flops 4224 | bytes 33792 | tf_op jit(solution)/shard_map/psum | solution.py:172
  1015.0 17.5 %all-reduce.5 = (f32[8,16]{1,0:T(8,128)}, f32[2048]{0:T(1024)}, f32[2048]{0:T(1024)}) all-reduce(f32[8,16]{1,0:T(8,128)S(1)} %get-tuple-element.359, f32[2048]{0:T(1024)S(1)} %get-tuple-element.360, f32[2048]{0:T(1024)S(1)} %get-tuple-element.361), channel_id=1, replica_groups=mesh['dp'=4,'ctx'=64,'mp'=2] {'dp'}, use_global_device_ids=true, to_apply=%region_26.27 | all-reduce | flops 4224 | bytes 33792 | tf_op jit(solution)/shard_map/psum | solution.py:171
  1032.5 3.5 fusion.57
  1036.0 41.1 %all-reduce.13.cloned.1.call-done = (f32[7,3,2048]{2,1,0:T(4,128)}, f32[8,2048]{1,0:T(8,128)}) async-done(((f32[7,3,2048]{2,1,0:T(4,128)}, f32[8,2048]{1,0:T(8,128)}), (f32[7,3,2048]{2,1,0:T(4,128)}, f32[8,2048]{1,0:T(8,128)})) %all-reduce.13.cloned.1.call-update) | async-done | bytes 237584 | tf_op jit(solution)/shard_map/psum | solution.py:171
  1077.1 1.7 copy.61
  1078.8 1.5 copy.152
  (570 shorter events, 217.5 us)
Async XLA Ops:
  7.2 216.1 %all-gather.7.cloned.1.call-start = ((), (), s32[]{:S(2)}) async-start(), calls=%async_computation | async-start | bytes 4259840 | tf_op jit(solution)/shard_map/all_gather | solution.py:21
  8.1 4.2 collective-permute-start
  11.3 10.0 copy-start.6
  11.3 10.0 copy-start.7
  11.4 9.9 copy-start.8
  11.4 9.9 copy-start.9
  11.4 9.9 copy-start.10
  11.5 9.9 copy-start.11
  12.2 9.2 copy-start.12
  22.8 1.0 copy-start.1
  63.2 10.0 copy-start.18
  63.2 10.7 copy-start.17
  73.8 414.8 %all-gather.9.cloned.1.call-start = ((), (), s32[]{:S(2)}) async-start(), calls=%async_computation.1 | async-start | bytes 4259840 | tf_op jit(solution)/shard_map/all_gather | solution.py:21
  73.9 94.6 %copy-start.4 = (f32[16,8,16,128]{3,1,2,0:T(8,128)S(1)}, f32[16,8,16,128]{3,1,2,0:T(8,128)}, u32[]{:S(2)}) copy-start(f32[16,8,16,128]{3,1,2,0:T(8,128)} %get-tuple-element.387) | copy-start | bytes 3145732
  75.2 148.1 %copy-start.15 = (f32[8,2048]{1,0:T(8,128)S(1)}, f32[8,2048]{1,0:T(8,128)}, u32[]{:S(2)}) copy-start(f32[8,2048]{1,0:T(8,128)} %param.18) | copy-start | bytes 196612
  223.3 9.2 copy-start.2
  223.3 9.2 copy-start.14
  223.3 9.2 copy-start.16
  237.8 13.6 %copy-start.19 = (f32[128]{0:T(128)}, f32[128]{0:T(128)S(1)}, u32[]{:S(2)}) copy-start(f32[128]{0:T(128)S(1)} %get-tuple-element.398) | copy-start | bytes 1540
  241.0 1.1 copy-start.3
  243.7 788.8 %all-reduce.11.cloned.1.call-start = ((), (), s32[]{:S(2)}) async-start(), calls=%async_computation.2 | async-start | bytes 589824 | tf_op jit(solution)/shard_map/psum | solution.py:172
  251.4 2.9 copy-start.5
  710.8 7.9 copy-start.13
  710.8 5.2 copy-start.20
  718.8 2.0 copy-start
  729.1 348.0 %all-reduce.13.cloned.1.call-start = ((), (), s32[]{:S(2)}) async-start(), calls=%async_computation.3 | async-start | bytes 589824 | tf_op jit(solution)/shard_map/psum | solution.py:171
  737.0 295.5 %collective-permute-start.1 = (f32[6,3,2048]{2,0,1:T(8,128)S(1)}, f32[6,3,2048]{2,0,1:T(8,128)S(1)}, u32[]{:S(2)}, u32[]{:S(2)}) collective-permute-start(f32[6,3,2048]{2,0,1:T(8,128)S(1)} %slice.156), channel_id=1, source_target_pairs={{2,0},{4,2},{6,4},{8,6},{10,8},{12,10},{14,12},{16,14},{18,16},{20... | collective-permute-start | bytes 442376 | tf_op jit(solution)/shard_map/ppermute | solution.py:14
Sparse Core Ops, SparseCore 0:
  73.9 149.2 all-gather.6
  243.9 244.6 all-gather.8
  729.2 251.4 all-reduce.10
  1032.6 44.4 all-reduce.12
